TPU v7x, 32 devices: a whole 2x2x4 slice. The times are simulated.
32 devices in a mesh: dp: 4 (over y, x), expert: 8 (over z, core).
Axes of the slice: x: 2, y: 2, z: 4, core: 2. Of those that a mesh axis runs over, the one named last changes fastest.
Arguments:
- latent: bfloat16 [4096, 512], P(('dp', 'expert')), may hold values from -6 to 6
- up_proj: bfloat16 [512, 4096], P(None, 'expert'), may hold values from -0.25 to 0.25
- expert_in: bfloat16 [8, 512, 4096], P('expert'), may hold values from -0.25 to 0.25
- expert_out: bfloat16 [8, 2048, 512], P('expert'), may hold values from -0.125 to 0.125
- routes: int32 [4096, 8], P(('dp', 'expert')), may hold values from 0 to 127, all different within a row; in each aligned block of 128 rows (0 to 127, 128 to 255, ...) at most 13 rows name the same one
- gates: bfloat16 [4096, 8], P(('dp', 'expert')), may hold values from 0.099609375 to 1
- cotangent: bfloat16 [4096, 4096], P('dp', 'expert'), may hold values from -6 to 6
Outputs:
- mixed: bfloat16 [4096, 4096], P('dp', 'expert')
- grad_up: float32 [512, 4096], P(None, 'expert')
Inputs may be any that keep to these rules, and one draw needn't show every extreme that they name: `routes`: in each aligned block of 128 rows (the tokens of one device) no expert is named more than 13 times.
All inputs are finite; a program needn't handle non-finite values.
Results may differ from a plain program's by a relative error of at most 0.0064.
Values may be sent and summed in bfloat16 or wider, within the bound.
A program may use at most 64 MiB of HBM per device.

v0:
```python
import jax
import jax.numpy as jnp
from jax import lax
from jax.sharding import PartitionSpec as P

TOP = 8
CAP = 13


def body(latent, up_proj, expert_in, expert_out, routes, gates, cotangent):
    n_expert = lax.axis_size("expert")
    tok_dev = routes.shape[0]
    width = latent.shape[1]
    hidden = expert_out.shape[1]
    flat = routes.reshape(-1)
    inside = flat < n_expert
    onehot = (flat[:, None] == jnp.arange(n_expert, dtype=jnp.int32)[None, :]).astype(jnp.int32)
    before = jnp.cumsum(onehot, axis=0) - onehot
    slot = jnp.sum(before * onehot, axis=1)
    target = jnp.where(inside, flat * CAP + slot, -1)
    place = (jnp.arange(n_expert * CAP, dtype=jnp.int32)[:, None] == target[None, :]).astype(
        jnp.float32
    )
    owner = (
        jnp.arange(flat.shape[0], dtype=jnp.int32)[:, None] // TOP
        == jnp.arange(tok_dev, dtype=jnp.int32)[None, :]
    ).astype(jnp.float32)
    dispatch = jnp.dot(place, owner, precision=lax.Precision.HIGHEST).astype(jnp.bfloat16)
    weighted = owner * gates.reshape(-1).astype(jnp.float32)[:, None]
    weighting = jnp.dot(weighted.T, place.T, precision=lax.Precision.HIGHEST).astype(jnp.bfloat16)
    outgoing = jnp.dot(dispatch, latent, preferred_element_type=jnp.float32).astype(jnp.bfloat16)
    outgoing = outgoing.reshape(n_expert, CAP, width)
    arrived = lax.all_to_all(outgoing, "expert", split_axis=0, concat_axis=0, tiled=True)
    rows = arrived.reshape(-1, width)
    gated = jnp.dot(rows, expert_in[0], preferred_element_type=jnp.float32)
    act = (jax.nn.silu(gated[:, :hidden]) * gated[:, hidden:]).astype(jnp.bfloat16)
    result = jnp.dot(act, expert_out[0], preferred_element_type=jnp.float32).astype(jnp.bfloat16)
    produced = result.reshape(arrived.shape)
    back = lax.all_to_all(produced, "expert", split_axis=0, concat_axis=0, tiled=True)
    own_rows = jnp.dot(
        weighting, back.reshape(-1, width), preferred_element_type=jnp.float32
    ).astype(jnp.bfloat16)
    combined = lax.all_gather(own_rows, "expert", axis=0, tiled=True)
    mixed = jnp.dot(combined, up_proj, preferred_element_type=jnp.float32).astype(jnp.bfloat16)
    partial_grad = jnp.einsum("tl,td->ld", combined, cotangent, preferred_element_type=jnp.float32)
    grad_up = lax.psum(partial_grad, "dp")
    return (mixed, grad_up)


def solution(mesh):
    in_specs = (
        P(("dp", "expert"), None),
        P(None, "expert"),
        P("expert", None, None),
        P("expert", None, None),
        P(("dp", "expert"), None),
        P(("dp", "expert"), None),
        P("dp", "expert"),
    )
    out_specs = (P("dp", "expert"), P(None, "expert"))
    return jax.shard_map(body, mesh=mesh, in_specs=in_specs, out_specs=out_specs, check_vma=False)
```

profile of v0, /device:TPU:0, one launch (start us, length us, event | category | flops | bytes accessed | tf_op | source)
XLA Modules:
  0.0 127.9 jit_solution(1610134031385471320)
XLA Ops:
  7.2 0.0 copy-start
  7.2 0.9 copy.10
  8.1 0.1 reshape.94
  8.2 0.1 eq.62
  8.3 2.3 %reduce-window.6 = s32[8,8,128]{2,1,0:T(8,128)S(1)} reduce-window(s32[8,8,128]{2,1,0:T(8,128)S(1)} %fusion.20, s32[]{:T(128)} %constant.26.clone.1), window={size=1x1x128 pad=0_0x0_0x127_0}, to_apply=%region_0.0 | reduce-window | flops 1040384 | bytes 65540 | tf_op jit(solution)/shard_map/reduce-window
  10.6 0.3 slice_reduce_fusion
  10.9 0.2 reduce-window.9
  11.0 0.1 add_bitcast_fusion
  11.2 0.4 convolution_convert_fusion.4
  11.5 1.1 convolution_convert_fusion.2
  12.6 0.7 reshape.96
  13.3 6.3 %all-to-all-start = ((bf16[8,13,512]{2,1,0:T(8,128)(2,1)}), bf16[8,13,512]{2,1,0:T(8,128)(2,1)S(1)}, u32[]{:S(2)}, u32[]{:S(2)}) async-start(bf16[8,13,512]{2,1,0:T(8,128)(2,1)} %reshape.96), calls=%async_computation | async-start | bytes 262144 | tf_op jit(solution)/shard_map/all_to_all | solution.py:33
  19.6 0.8 copy.9
  20.4 0.1 reshape.100
  20.5 5.9 %all-to-all-done = bf16[8,13,512]{2,1,0:T(8,128)(2,1)S(1)} async-done(((bf16[8,13,512]{2,1,0:T(8,128)(2,1)}), bf16[8,13,512]{2,1,0:T(8,128)(2,1)S(1)}, u32[]{:S(2)}, u32[]{:S(2)}) %all-to-all-start) | async-done | bytes 106528 | tf_op jit(solution)/shard_map/all_to_all | solution.py:33
  26.5 2.9 %fusion = f32[104,4096]{1,0:T(8,128)S(1)} fusion(bf16[104,512]{1,0:T(8,128)(2,1)S(1)} %reshape.97, bf16[1,512,4096]{2,1,0:T(8,128)(2,1)} %param.9), kind=kOutput, calls=%fused_computation | convolution fusion | flops 436207616 | bytes 6004736 | tf_op jit(solution)/shard_map/dot_general | solution.py:35
  29.4 0.0 copy-done
  29.4 0.0 copy-start.1
  29.4 0.5 fusion.4
  30.0 0.7 reshape.98
  30.7 3.4 %all-to-all-start.1 = ((bf16[8,13,512]{2,1,0:T(8,128)(2,1)}), bf16[8,13,512]{2,1,0:T(8,128)(2,1)S(1)}, u32[]{:S(2)}, u32[]{:S(2)}) async-start(bf16[8,13,512]{2,1,0:T(8,128)(2,1)} %reshape.98), calls=%async_computation.1 | async-start | bytes 262144 | tf_op jit(solution)/shard_map/all_to_all | solution.py:39
  34.1 0.0 all-gather.2.cloned.1.call-start
  34.1 0.9 convolution_convert_fusion.3
  35.0 5.8 %all-to-all-done.1 = bf16[8,13,512]{2,1,0:T(8,128)(2,1)S(1)} async-done(((bf16[8,13,512]{2,1,0:T(8,128)(2,1)}), bf16[8,13,512]{2,1,0:T(8,128)(2,1)S(1)}, u32[]{:S(2)}, u32[]{:S(2)}) %all-to-all-start.1) | async-done | bytes 106528 | tf_op jit(solution)/shard_map/all_to_all | solution.py:39
  40.8 0.8 convolution_convert_fusion.1
  41.7 0.0 all-gather.2.cloned.1.call-update
  41.7 0.0 all-reduce.2.cloned.1.call-start
  41.7 21.2 %all-gather.2.cloned.1.call-done = bf16[1024,512]{1,0:T(8,128)(2,1)} async-done(((bf16[128,512]{1,0:T(8,128)(2,1)}), bf16[1024,512]{1,0:T(8,128)(2,1)}) %all-gather.2.cloned.1.call-update) | async-done | bytes 1048592 | tf_op jit(solution)/shard_map/all_gather | solution.py:43
  63.0 0.0 copy-done.1
  63.0 2.9 %fusion.26 = f32[512,512]{1,0:T(8,128)} fusion(bf16[1024,512]{1,0:T(8,128)(2,1)} %all-gather.2.cloned.1.call-done, bf16[1024,512]{1,0:T(8,128)(2,1)S(1)} %copy-done.1), kind=kOutput, calls=%fused_computation.41 | convolution fusion | flops 536870912 | bytes 3145728 | tf_op jit(solution)/shard_map/tl,td->ld/dot_general | solution.py:45
  65.9 0.0 all-reduce.2.cloned.1.call-update
  65.9 3.0 %convolution_convert_fusion = bf16[1024,512]{1,0:T(8,128)(2,1)} fusion(bf16[1024,512]{1,0:T(8,128)(2,1)} %all-gather.2.cloned.1.call-done, bf16[512,512]{1,0:T(8,128)(2,1)} %param.8), kind=kOutput, calls=%fused_computation.4 | convolution fusion | flops 537395200 | bytes 2621440 | tf_op jit(solution)/shard_map/dot_general | solution.py:44
  69.0 49.9 %all-reduce.2.cloned.1.call-done = f32[512,512]{1,0:T(8,128)} async-done(((f32[512,512]{1,0:T(8,128)}), f32[512,512]{1,0:T(8,128)}) %all-reduce.2.cloned.1.call-update) | async-done | bytes 1048592 | tf_op jit(solution)/shard_map/psum | solution.py:46
  118.8 2.3 %copy.15 = f32[512,512]{1,0:T(8,128)} copy(f32[512,512]{1,0:T(8,128)} %all-reduce.2.cloned.1.call-done) | data formatting | bytes 2097152
  (5 shorter events, 0.1 us)
Async XLA Ops:
  7.2 22.3 %copy-start = (bf16[1,2048,512]{2,1,0:T(8,128)(2,1)S(1)}, bf16[1,2048,512]{2,1,0:T(8,128)(2,1)}, u32[]{:S(2)}) copy-start(bf16[1,2048,512]{2,1,0:T(8,128)(2,1)} %param.10) | copy-start | bytes 6291460
  13.3 13.1 %all-to-all-start = ((bf16[8,13,512]{2,1,0:T(8,128)(2,1)}), bf16[8,13,512]{2,1,0:T(8,128)(2,1)S(1)}, u32[]{:S(2)}, u32[]{:S(2)}) async-start(bf16[8,13,512]{2,1,0:T(8,128)(2,1)} %reshape.96), calls=%async_computation | async-start | bytes 262144 | tf_op jit(solution)/shard_map/all_to_all | solution.py:33
  29.4 33.6 %copy-start.1 = (bf16[1024,512]{1,0:T(8,128)(2,1)S(1)}, bf16[1024,512]{1,0:T(8,128)(2,1)}, u32[]{:S(2)}) copy-start(bf16[1024,512]{1,0:T(8,128)(2,1)} %param.13) | copy-start | bytes 3145732
  30.7 10.1 %all-to-all-start.1 = ((bf16[8,13,512]{2,1,0:T(8,128)(2,1)}), bf16[8,13,512]{2,1,0:T(8,128)(2,1)S(1)}, u32[]{:S(2)}, u32[]{:S(2)}) async-start(bf16[8,13,512]{2,1,0:T(8,128)(2,1)} %reshape.98), calls=%async_computation.1 | async-start | bytes 262144 | tf_op jit(solution)/shard_map/all_to_all | solution.py:39
  34.1 28.9 %all-gather.2.cloned.1.call-start = ((), (), s32[]{:S(2)}) async-start(), calls=%async_computation.2 | async-start | bytes 1179648 | tf_op jit(solution)/shard_map/all_gather | solution.py:43
  41.7 77.1 %all-reduce.2.cloned.1.call-start = ((), (), s32[]{:S(2)}) async-start(), calls=%async_computation.3 | async-start | bytes 2097152 | tf_op jit(solution)/shard_map/psum | solution.py:46
Sparse Core Ops, SparseCore 0:
  41.8 21.1 all-gather.1
  66.6 52.1 all-reduce.1
where the time goes:
time: 128 us
  waiting for transfers between devices  82.8 us (65%)
  between operations  14.1 us (11%)
  matrix products  12.6 us (10%)
  starting transfers between devices  9.78 us (8%)
  local copies, waits for them, and re-layouts  6.07 us (5%)
  other arithmetic  2.55 us (2%)
    psum x1, waiting for transfers between devices, body(): grad_up = lax.psum(partial_grad, 'dp')  49.9 us
    all_gather x1, waiting for transfers between devices, body(): combined = lax.all_gather(own_rows, 'expert', axis=0, tiled=True)  21.2 us
    all_to_all x1, starting transfers between devices, body(): lax.all_to_all(outgoing, 'expert', split_axis=0, concat_axis=0, tiled=True)  6.32 us
    all_to_all x1, waiting for transfers between devices, body(): lax.all_to_all(outgoing, 'expert', split_axis=0, concat_axis=0, tiled=True)  5.91 us
    all_to_all x1, waiting for transfers between devices, body(): lax.all_to_all(produced, 'expert', split_axis=0, concat_axis=0, tiled=True)  5.78 us
    all_to_all x1, starting transfers between devices, body(): lax.all_to_all(produced, 'expert', split_axis=0, concat_axis=0, tiled=True)  3.37 us
    unnamed x6, local copies, waits for them, and re-layouts  3.21 us
    dot_general x1, matrix products, body(): jnp.dot(combined, up_proj, preferred_element_type=jnp.float32)  3.03 us
  transfers between devices with their start and end apart: 4, of which 4 were waited for; matrix products, arithmetic and copies ran while one was open for 4% of the time, Pallas kernels for 0%

commit v1 on v0

v1 whole, which is shorter than its diff:
```python
import functools

import jax
import jax.numpy as jnp
from jax import lax
from jax.experimental import pallas as pl
from jax.experimental.pallas import tpu as pltpu
from jax.sharding import PartitionSpec as P

MESH = pl.DeviceIdType.MESH
SLOTS = 16
CORES = 2


def each(count, step):
    if count <= 8:
        for i in range(count):
            step(i)
    else:
        lax.fori_loop(0, count, lambda i, carry: (step(i), carry)[1], 0)


def kernel(
    n_e, n_dp, chunks,
    routes_ref, gates_ref, latent_ref, up_hbm, win_hbm, wout_hbm, cot_hbm,
    mixed_hbm, grad_hbm,
    win, wout, cot, up, dsend, drecv, act, rsend, gbuf, weight, comb, mixed, gsend, rsbuf, asend,
    load_sem, d_send, d_recv, g_send, g_recv, f_send, r_send, r_recv, a_send, a_recv, own_sem, out_sem,
):
    me = lax.axis_index("expert")
    dp = lax.axis_index("dp")
    n_z = n_e // CORES
    z, core = me // CORES, lax.rem(me, CORES)
    sibling = z * CORES + (CORES - 1 - core)
    z_peers = [lax.rem(z + off, n_z) * CORES + core for off in range(1, n_z)]
    f_peers = [lax.rem(z + off, n_z) * CORES + (CORES - 1 - core) for off in range(1, n_z)]
    e_peers = [lax.rem(me + off, n_e) for off in range(1, n_e)]
    dp_peers = [lax.rem(dp + off, n_dp) for off in range(1, n_dp)]

    barrier = pltpu.get_barrier_semaphore()
    for peer in e_peers:
        pl.semaphore_signal(barrier, inc=1, device_id={"expert": peer}, device_id_type=MESH)
    for peer in dp_peers:
        pl.semaphore_signal(barrier, inc=1, device_id={"dp": peer}, device_id_type=MESH)

    loads = [
        pltpu.make_async_copy(src, dst, load_sem.at[i])
        for i, (src, dst) in enumerate(
            ((win_hbm.at[0], win), (wout_hbm.at[0], wout), (cot_hbm, cot), (up_hbm, up))
        )
    ]
    for load in loads:
        load.start()

    tok = latent_ref.shape[0]
    width = latent_ref.shape[1]
    hidden = wout.shape[0]
    top = routes_ref.shape[0]
    rows = n_e * SLOTS
    cols = width // chunks
    share = cols // n_dp
    meta_parts = (2 * n_e) // SLOTS

    expert_of = lax.broadcasted_iota(jnp.int32, (n_e, tok), 0)
    named = jnp.zeros((n_e, tok), jnp.float32)
    gate = jnp.zeros((n_e, tok), jnp.float32)
    for k in range(top):
        hit = routes_ref[k : k + 1, :] == expert_of
        named = jnp.where(hit, 1.0, named)
        gate = jnp.where(hit, gates_ref[k : k + 1, :].astype(jnp.float32), gate)
    earlier = lax.broadcasted_iota(jnp.int32, (tok, tok), 0) < lax.broadcasted_iota(
        jnp.int32, (tok, tok), 1
    )
    before = jnp.dot(
        named.astype(jnp.bfloat16),
        jnp.where(earlier, 1.0, 0.0).astype(jnp.bfloat16),
        preferred_element_type=jnp.float32,
    )
    slot = jnp.where(named > 0.0, before, -1.0)
    slot_of = lax.broadcasted_iota(jnp.int32, (SLOTS, tok), 0).astype(jnp.float32)
    pick = jnp.concatenate(
        [jnp.where(slot[e : e + 1, :] == slot_of, 1.0, 0.0) for e in range(n_e)], axis=0
    ).astype(jnp.bfloat16)
    outgoing = jnp.dot(pick, latent_ref[...], preferred_element_type=jnp.float32)
    dsend[:, :, :width] = outgoing.astype(jnp.bfloat16).reshape(n_e, SLOTS, width)
    meta = jnp.concatenate([slot, gate], axis=0).astype(jnp.bfloat16)
    for j in range(meta_parts):
        part = meta[j * SLOTS : (j + 1) * SLOTS, :]
        dsend[:, :, width + j * tok : width + (j + 1) * tok] = jnp.broadcast_to(
            part[None], (n_e, SLOTS, tok)
        )
    drecv[me] = dsend[me]

    pl.semaphore_wait(barrier, n_e - 1 + n_dp - 1)

    def dispatch(slot_, peer):
        return pltpu.make_async_remote_copy(
            src_ref=dsend.at[peer], dst_ref=drecv.at[slot_],
            send_sem=d_send.at[peer], recv_sem=d_recv.at[slot_],
            device_id={"expert": peer}, device_id_type=MESH,
        )

    for peer in e_peers:
        dispatch(me, peer).start()
    loads[0].wait()
    for peer in e_peers:
        dispatch(peer, peer).wait_recv()

    arrived = drecv[:, :, :width].reshape(rows, width)
    tile = min(512, hidden)
    for j in range(hidden // tile):
        g = jnp.dot(arrived, win[:, j * tile : (j + 1) * tile], preferred_element_type=jnp.float32)
        u = jnp.dot(
            arrived, win[:, hidden + j * tile : hidden + (j + 1) * tile],
            preferred_element_type=jnp.float32,
        )
        act[:, j * tile : (j + 1) * tile] = (g / (1.0 + jnp.exp(-g)) * u).astype(jnp.bfloat16)

    def gather(c, source, peer, peer_slot, src, sems):
        return pltpu.make_async_remote_copy(
            src_ref=src, dst_ref=gbuf.at[c, source],
            send_sem=sems.at[c, peer_slot], recv_sem=g_recv.at[c, source],
            device_id={"expert": peer}, device_id_type=MESH,
        )

    loads[1].wait()
    sends = []
    for c in range(chunks):
        result = jnp.dot(
            act[...], wout[:, c * cols : (c + 1) * cols], preferred_element_type=jnp.float32
        ).astype(jnp.bfloat16)
        rsend[c] = result
        for i, peer in enumerate(z_peers + [sibling]):
            copy = gather(c, me, peer, i, rsend.at[c], g_send)
            copy.start()
            sends.append(copy)
        gbuf[c, me] = result

    def weigh(b):
        both = jnp.concatenate(
            [drecv[b, :, width + j * tok : width + (j + 1) * tok] for j in range(meta_parts)], axis=0
        ).astype(jnp.float32)
        spread = jnp.concatenate(
            [
                jnp.where(both[e : e + 1, :] == slot_of, both[n_e + e : n_e + e + 1, :], 0.0)
                for e in range(n_e)
            ],
            axis=0,
        )
        weight[b] = spread.T.astype(jnp.bfloat16)

    each(n_e, weigh)
    loads[2].wait()

    def scatter(c, slot_, peer):
        return pltpu.make_async_remote_copy(
            src_ref=gsend.at[c, peer], dst_ref=rsbuf.at[c, slot_],
            send_sem=r_send.at[c, peer], recv_sem=r_recv.at[c, slot_],
            device_id={"dp": peer}, device_id_type=MESH,
        )

    def spread_sum(c, slot_, peer):
        return pltpu.make_async_remote_copy(
            src_ref=asend.at[c], dst_ref=grad_hbm.at[c, slot_],
            send_sem=a_send.at[c, peer], recv_sem=a_recv.at[c, slot_],
            device_id={"dp": peer}, device_id_type=MESH,
        )

    def own_sum(c):
        return pltpu.make_async_copy(asend.at[c], grad_hbm.at[c, dp], own_sem.at[c])

    def reduce(c):
        total = gsend[c, dp].astype(jnp.float32)
        for peer in dp_peers:
            scatter(c, peer, peer).wait_recv()
            total = total + rsbuf[c, peer].astype(jnp.float32)
        asend[c] = total.astype(jnp.bfloat16)
        for peer in dp_peers:
            spread_sum(c, dp, peer).start()
        own_sum(c).start()

    for c in range(chunks):
        for i, peer in enumerate(z_peers):
            gather(c, peer, peer, i, rsend.at[c], g_send).wait_recv()
            forward = gather(c, peer, sibling, i, gbuf.at[c, peer], f_send)
            forward.start()
            sends.append(forward)
        gather(c, sibling, sibling, n_z - 1, rsend.at[c], g_send).wait_recv()
        for i, peer in enumerate(f_peers):
            gather(c, peer, sibling, i, rsend.at[c], f_send).wait_recv()

        def combine(b):
            at = b * SLOTS
            found = gbuf[c, :, pl.ds(at, SLOTS), :].reshape(rows, cols)
            comb[pl.ds(b * tok, tok), c * cols : (c + 1) * cols] = jnp.dot(
                weight[b], found, preferred_element_type=jnp.float32
            ).astype(jnp.bfloat16)

        each(n_e, combine)
        partial = lax.dot_general(
            comb[:, c * cols : (c + 1) * cols], cot[...], (((0,), (0,)), ((), ())),
            preferred_element_type=jnp.float32,
        )
        gsend[c] = partial.astype(jnp.bfloat16).reshape(n_dp, share, cot.shape[1])
        for peer in dp_peers:
            scatter(c, dp, peer).start()
        if c > 0:
            reduce(c - 1)

    loads[3].wait()

    def project(b):
        at = pl.ds(b * tok, tok)
        mixed[at, :] = jnp.dot(
            comb[at, :], up[...], preferred_element_type=jnp.float32
        ).astype(jnp.bfloat16)

    each(n_e, project)
    out = pltpu.make_async_copy(mixed, mixed_hbm, out_sem)
    out.start()
    reduce(chunks - 1)

    for peer in e_peers:
        dispatch(me, peer).wait_send()
    for copy in sends:
        copy.wait_send()
    for c in range(chunks):
        for peer in dp_peers:
            scatter(c, dp, peer).wait_send()
            spread_sum(c, dp, peer).wait_send()
            spread_sum(c, peer, peer).wait_recv()
        own_sum(c).wait()
    out.wait()


def body(n_e, n_dp, latent, up_proj, expert_in, expert_out, routes, gates, cotangent):
    tok, width = latent.shape
    hidden = expert_out.shape[1]
    group, features = cotangent.shape
    chunks = max(1, min(4, width // (16 * n_dp)))
    cols = width // chunks
    share = cols // n_dp
    rows = n_e * SLOTS
    n_z = n_e // CORES
    wide = width + (2 * n_e // SLOTS) * tok
    vmem = pl.BlockSpec(memory_space=pltpu.VMEM)
    hbm = pl.BlockSpec(memory_space=pl.ANY)
    bf16 = jnp.bfloat16
    dma = pltpu.SemaphoreType.DMA
    mixed, grad = pl.pallas_call(
        functools.partial(kernel, n_e, n_dp, chunks),
        out_shape=(
            jax.ShapeDtypeStruct((group, features), bf16),
            jax.ShapeDtypeStruct((chunks, n_dp, share, features), bf16),
        ),
        in_specs=[vmem, vmem, vmem, hbm, hbm, hbm, hbm],
        out_specs=(hbm, hbm),
        scratch_shapes=[
            pltpu.VMEM((width, 2 * hidden), bf16),
            pltpu.VMEM((hidden, width), bf16),
            pltpu.VMEM((group, features), bf16),
            pltpu.VMEM((width, features), bf16),
            pltpu.VMEM((n_e, SLOTS, wide), bf16),
            pltpu.VMEM((n_e, SLOTS, wide), bf16),
            pltpu.VMEM((rows, hidden), bf16),
            pltpu.VMEM((chunks, rows, cols), bf16),
            pltpu.VMEM((chunks, n_e, rows, cols), bf16),
            pltpu.VMEM((n_e, tok, rows), bf16),
            pltpu.VMEM((group, width), bf16),
            pltpu.VMEM((group, features), bf16),
            pltpu.VMEM((chunks, n_dp, share, features), bf16),
            pltpu.VMEM((chunks, n_dp, share, features), bf16),
            pltpu.VMEM((chunks, share, features), bf16),
            dma((4,)),
            dma((n_e,)),
            dma((n_e,)),
            dma((chunks, n_z)),
            dma((chunks, n_e)),
            dma((chunks, n_z)),
            dma((chunks, n_dp)),
            dma((chunks, n_dp)),
            dma((chunks, n_dp)),
            dma((chunks, n_dp)),
            dma((chunks,)),
            dma,
        ],
        compiler_params=pltpu.CompilerParams(
            collective_id=0, has_side_effects=True, vmem_limit_bytes=56 * 1024 * 1024
        ),
        cost_estimate=pl.CostEstimate(
            flops=2 * rows * width * hidden * 3 + 4 * group * width * features,
            bytes_accessed=6 * hidden * width + 8 * group * features,
            transcendentals=rows * hidden,
        ),
    )(routes.T, gates.T, latent, up_proj, expert_in, expert_out, cotangent)
    return mixed, grad.reshape(width, features).astype(jnp.float32)


def solution(mesh):
    in_specs = (
        P(("dp", "expert"), None),
        P(None, "expert"),
        P("expert", None, None),
        P("expert", None, None),
        P(("dp", "expert"), None),
        P(("dp", "expert"), None),
        P("dp", "expert"),
    )
    out_specs = (P("dp", "expert"), P(None, "expert"))
    return jax.shard_map(
        functools.partial(body, mesh.shape["expert"], mesh.shape["dp"]),
        mesh=mesh, in_specs=in_specs, out_specs=out_specs, check_vma=False,
    )
```

time: 128 us -> 41.7 us (0.33)
  waiting for transfers between devices: 82.8 us -> 0 us
  Pallas kernels: 0 us -> 36.4 us
  between operations: 14.1 us -> 0.64 us
  matrix products: 12.6 us -> 0 us
  starting transfers between devices: 9.78 us -> 0 us
  local copies, waits for them, and re-layouts: 6.07 us -> 2.26 us
    psum x1 -> x0, waiting for transfers between devices: 49.9 us -> none  [body(): grad_up = lax.psum(partial_grad, 'dp')]
    pallas_call x0 -> x1, Pallas kernels: none -> 36.4 us  [body(): pl.pallas_call(functools.partial(kernel, n_e, n_dp, chunks), out_shape=(j...]
    all_gather x1 -> x0, waiting for transfers between devices: 21.2 us -> none  [body(): combined = lax.all_gather(own_rows, 'expert', axis=0, tiled=True)]
    dot_general x8 -> x0, matrix products: 12.6 us -> none  [the longest x1 3.03 us: body(): jnp.dot(combined, up_proj, preferred_element_type=jnp.float32)]
    all_to_all x2 -> x0, waiting for transfers between devices: 11.7 us -> none  [the longest x1 5.91 us: body(): lax.all_to_all(outgoing, 'expert', split_axis=0, concat_axis=0, tiled=True)]
    all_to_all x2 -> x0, starting transfers between devices: 9.69 us -> none  [the longest x1 6.32 us: body(): lax.all_to_all(outgoing, 'expert', split_axis=0, concat_axis=0, tiled=True)]
    another operation x2 -> x0, other arithmetic: 2.43 us -> none
    convert_element_type x1, other arithmetic: 0.01 us -> 2.15 us  [body(): return (mixed, grad.reshape(width, features).astype(jnp.float32))]
  transfers between devices with their start and end apart: 4 -> 0, of which waited for: 4 -> 0; matrix products, arithmetic and copies ran while one was open for 4% -> 0% of each run, Pallas kernels for 0% -> 0%
where the time goes in v1:
time: 41.7 us; the launch traced here: 41.4 us
  Pallas kernels  36.4 us (87%)
  local copies, waits for them, and re-layouts  2.26 us (5%)
  other arithmetic  2.15 us (5%)
  between operations  0.64 us (2%)
    pallas_call x1, Pallas kernels, body(): pl.pallas_call(functools.partial(kernel, n_e, n_dp, chunks), out_shape=(j...  36.4 us
    unnamed x1, local copies, waits for them, and re-layouts  2.26 us
    convert_element_type x1, other arithmetic, body(): return (mixed, grad.reshape(width, features).astype(jnp.float32))  2.15 us

profile of v1, /device:TPU:0, one launch (start us, length us, event | category | flops | bytes accessed | tf_op | source)
XLA Modules:
  0.0 41.4 jit_solution(17191118108940651882)
XLA Ops:
  0.6 36.4 %shard_map.86 = (bf16[1024,512]{1,0:T(8,128)(2,1)}, bf16[4,4,32,512]{3,2,1,0:T(8,128)(2,1)}) custom-call(s32[8,128]{1,0:T(8,128)} %bitcast.5, bf16[8,128]{1,0:T(8,128)(2,1)} %bitcast.6, bf16[128,512]{1,0:T(8,128)(2,1)} %latent_ref.1, bf16[512,512]{1,0:T(8,128)(2,1)} %up_hbm.1, bf16[1,512,4096]{2,1,0:T(8,128)(2,1)} %win_hbm.1, ...), custom_call_target="tpu_custom_call" | custom-call | flops 1879048192 | bytes 10485760 | tf_op jit(solution)/shard_map/pallas_call | solution.py:250
  37.0 2.1 %bitcast_convert_fusion = f32[512,512]{1,0:T(8,128)} fusion(bf16[4,4,32,512]{3,2,1,0:T(8,128)(2,1)} %get-tuple-element.5), kind=kLoop, calls=%fused_computation | loop fusion | flops 262144 | bytes 1572864 | tf_op jit(solution)/shard_map/convert_element_type | solution.py:296
  39.2 2.3 %copy.10 = bf16[1024,512]{1,0:T(8,128)(2,1)} copy(bf16[1024,512]{1,0:T(8,128)(2,1)} %get-tuple-element.8) | data formatting | bytes 2097152

commit v2 on v1

--- a/solution.py
+++ b/solution.py
@@ -24,8 +24,8 @@
     n_e, n_dp, chunks,
     routes_ref, gates_ref, latent_ref, up_hbm, win_hbm, wout_hbm, cot_hbm,
     mixed_hbm, grad_hbm,
-    win, wout, cot, up, dsend, drecv, act, rsend, gbuf, weight, comb, mixed, gsend, rsbuf, asend,
-    load_sem, d_send, d_recv, g_send, g_recv, f_send, r_send, r_recv, a_send, a_recv, own_sem, out_sem,
+    win, wout, cot, up, dsend, drecv, msend, mrecv, act, rsend, gbuf, weight, comb, mixed, gsend, rsbuf, asend,
+    load_sem, d_send, d_recv, m_send, m_recv, g_send, g_recv, r_send, r_recv, a_send, a_recv, own_sem, out_sem,
 ):
     me = lax.axis_index("expert")
     dp = lax.axis_index("dp")
@@ -59,7 +59,6 @@
     rows = n_e * SLOTS
     cols = width // chunks
     share = cols // n_dp
-    meta_parts = (2 * n_e) // SLOTS
 
     expert_of = lax.broadcasted_iota(jnp.int32, (n_e, tok), 0)
     named = jnp.zeros((n_e, tok), jnp.float32)
@@ -82,13 +81,10 @@
         [jnp.where(slot[e : e + 1, :] == slot_of, 1.0, 0.0) for e in range(n_e)], axis=0
     ).astype(jnp.bfloat16)
     outgoing = jnp.dot(pick, latent_ref[...], preferred_element_type=jnp.float32)
-    dsend[:, :, :width] = outgoing.astype(jnp.bfloat16).reshape(n_e, SLOTS, width)
+    dsend[...] = outgoing.astype(jnp.bfloat16).reshape(n_e, SLOTS, width)
     meta = jnp.concatenate([slot, gate], axis=0).astype(jnp.bfloat16)
-    for j in range(meta_parts):
-        part = meta[j * SLOTS : (j + 1) * SLOTS, :]
-        dsend[:, :, width + j * tok : width + (j + 1) * tok] = jnp.broadcast_to(
-            part[None], (n_e, SLOTS, tok)
-        )
+    msend[...] = meta
+    mrecv[me] = meta
     drecv[me] = dsend[me]
 
     pl.semaphore_wait(barrier, n_e - 1 + n_dp - 1)
@@ -100,13 +96,22 @@
             device_id={"expert": peer}, device_id_type=MESH,
         )
 
+    def table(slot_, peer):
+        return pltpu.make_async_remote_copy(
+            src_ref=msend, dst_ref=mrecv.at[slot_],
+            send_sem=m_send.at[peer], recv_sem=m_recv.at[slot_],
+            device_id={"expert": peer}, device_id_type=MESH,
+        )
+
     for peer in e_peers:
         dispatch(me, peer).start()
+    for peer in e_peers:
+        table(me, peer).start()
     loads[0].wait()
     for peer in e_peers:
         dispatch(peer, peer).wait_recv()
 
-    arrived = drecv[:, :, :width].reshape(rows, width)
+    arrived = drecv[...].reshape(rows, width)
     tile = min(512, hidden)
     for j in range(hidden // tile):
         g = jnp.dot(arrived, win[:, j * tile : (j + 1) * tile], preferred_element_type=jnp.float32)
@@ -116,30 +121,59 @@
         )
         act[:, j * tile : (j + 1) * tile] = (g / (1.0 + jnp.exp(-g)) * u).astype(jnp.bfloat16)
 
-    def gather(c, source, peer, peer_slot, src, sems):
+    def gather(c, source, peer, sem, src):
         return pltpu.make_async_remote_copy(
             src_ref=src, dst_ref=gbuf.at[c, source],
-            send_sem=sems.at[c, peer_slot], recv_sem=g_recv.at[c, source],
+            send_sem=g_send.at[c, sem], recv_sem=g_recv.at[c, source],
             device_id={"expert": peer}, device_id_type=MESH,
         )
 
+    def landed(c, source):
+        gather(c, source, sibling, 0, gbuf.at[c, source]).wait_recv()
+
+    sends = []
+
+    def send(c, source, peer, sem, src):
+        copy = gather(c, source, peer, sem, src)
+        copy.start()
+        sends.append(copy)
+
+    relay = n_z == 4
+    near = (z + 1 - 2 * lax.rem(z, 2)) * CORES + core
+    over = lax.rem(z + 2, n_z) * CORES + core
+    far = (n_z - 1 - z) * CORES + core
+    direct = [over, near] if relay else z_peers
+
     loads[1].wait()
-    sends = []
     for c in range(chunks):
         result = jnp.dot(
             act[...], wout[:, c * cols : (c + 1) * cols], preferred_element_type=jnp.float32
         ).astype(jnp.bfloat16)
         rsend[c] = result
-        for i, peer in enumerate(z_peers + [sibling]):
-            copy = gather(c, me, peer, i, rsend.at[c], g_send)
-            copy.start()
-            sends.append(copy)
+        for i, peer in enumerate(direct + [sibling]):
+            send(c, me, peer, i, rsend.at[c])
         gbuf[c, me] = result
 
+    def first(c):
+        sem = len(direct) + 1
+        for peer in direct:
+            landed(c, peer)
+            if relay and peer is over:
+                send(c, peer, near, sem, gbuf.at[c, peer])
+                sem += 1
+            send(c, peer, sibling, sem, gbuf.at[c, peer])
+            sem += 1
+
+    def second(c):
+        if relay:
+            landed(c, far)
+            send(c, far, sibling, 2 * n_z - 2, gbuf.at[c, far])
+        landed(c, sibling)
+        for peer in f_peers:
+            landed(c, peer)
+
     def weigh(b):
-        both = jnp.concatenate(
-            [drecv[b, :, width + j * tok : width + (j + 1) * tok] for j in range(meta_parts)], axis=0
-        ).astype(jnp.float32)
+        both = mrecv[b].astype(jnp.float32)
         spread = jnp.concatenate(
             [
                 jnp.where(both[e : e + 1, :] == slot_of, both[n_e + e : n_e + e + 1, :], 0.0)
@@ -149,6 +183,8 @@
         )
         weight[b] = spread.T.astype(jnp.bfloat16)
 
+    for peer in e_peers:
+        table(peer, peer).wait_recv()
     each(n_e, weigh)
     loads[2].wait()
 
@@ -179,15 +215,11 @@
             spread_sum(c, dp, peer).start()
         own_sum(c).start()
 
+    first(0)
     for c in range(chunks):
-        for i, peer in enumerate(z_peers):
-            gather(c, peer, peer, i, rsend.at[c], g_send).wait_recv()
-            forward = gather(c, peer, sibling, i, gbuf.at[c, peer], f_send)
-            forward.start()
-            sends.append(forward)
-        gather(c, sibling, sibling, n_z - 1, rsend.at[c], g_send).wait_recv()
-        for i, peer in enumerate(f_peers):
-            gather(c, peer, sibling, i, rsend.at[c], f_send).wait_recv()
+        if c + 1 < chunks:
+            first(c + 1)
+        second(c)
 
         def combine(b):
             at = b * SLOTS
@@ -222,6 +254,7 @@
 
     for peer in e_peers:
         dispatch(me, peer).wait_send()
+        table(me, peer).wait_send()
     for copy in sends:
         copy.wait_send()
     for c in range(chunks):
@@ -233,6 +266,54 @@
     out.wait()
 
 
+def finish_kernel(parts, mixed_ref, grad_ref, mixed_out, grad_out, narrow, wide, copy_sem, in_sem, out_sem):
+    tall, deep = mixed_ref.shape[0] // parts, grad_ref.shape[0] // parts
+    copies, outs = [], []
+    ins = [
+        pltpu.make_async_copy(grad_ref.at[pl.ds(i * deep, deep)], narrow.at[i], in_sem.at[i])
+        for i in range(parts)
+    ]
+    for load in ins:
+        load.start()
+    for i in range(parts):
+        at = pl.ds(i * tall, tall)
+        copies.append(pltpu.make_async_copy(mixed_ref.at[at], mixed_out.at[at], copy_sem.at[i]))
+        copies[-1].start()
+    for i in range(parts):
+        ins[i].wait()
+        wide[i] = narrow[i].astype(jnp.float32)
+        outs.append(
+            pltpu.make_async_copy(wide.at[i], grad_out.at[pl.ds(i * deep, deep)], out_sem.at[i])
+        )
+        outs[-1].start()
+    for copy in copies + outs:
+        copy.wait()
+
+
+def finish(mixed, grad):
+    parts = 4
+    deep, features = grad.shape[0] // parts, grad.shape[1]
+    hbm = pl.BlockSpec(memory_space=pl.ANY)
+    dma = pltpu.SemaphoreType.DMA
+    return pl.pallas_call(
+        functools.partial(finish_kernel, parts),
+        out_shape=(
+            jax.ShapeDtypeStruct(mixed.shape, mixed.dtype),
+            jax.ShapeDtypeStruct(grad.shape, jnp.float32),
+        ),
+        in_specs=[hbm, hbm],
+        out_specs=(hbm, hbm),
+        scratch_shapes=[
+            pltpu.VMEM((parts, deep, features), jnp.bfloat16),
+            pltpu.VMEM((parts, deep, features), jnp.float32),
+            dma((parts,)),
+            dma((parts,)),
+            dma((parts,)),
+        ],
+        compiler_params=pltpu.CompilerParams(vmem_limit_bytes=56 * 1024 * 1024),
+    )(mixed, grad)
+
+
 def body(n_e, n_dp, latent, up_proj, expert_in, expert_out, routes, gates, cotangent):
     tok, width = latent.shape
     hidden = expert_out.shape[1]
@@ -242,7 +323,6 @@
     share = cols // n_dp
     rows = n_e * SLOTS
     n_z = n_e // CORES
-    wide = width + (2 * n_e // SLOTS) * tok
     vmem = pl.BlockSpec(memory_space=pltpu.VMEM)
     hbm = pl.BlockSpec(memory_space=pl.ANY)
     bf16 = jnp.bfloat16
@@ -260,8 +340,10 @@
             pltpu.VMEM((hidden, width), bf16),
             pltpu.VMEM((group, features), bf16),
             pltpu.VMEM((width, features), bf16),
-            pltpu.VMEM((n_e, SLOTS, wide), bf16),
-            pltpu.VMEM((n_e, SLOTS, wide), bf16),
+            pltpu.VMEM((n_e, SLOTS, width), bf16),
+            pltpu.VMEM((n_e, SLOTS, width), bf16),
+            pltpu.VMEM((2 * n_e, tok), bf16),
+            pltpu.VMEM((n_e, 2 * n_e, tok), bf16),
             pltpu.VMEM((rows, hidden), bf16),
             pltpu.VMEM((chunks, rows, cols), bf16),
             pltpu.VMEM((chunks, n_e, rows, cols), bf16),
@@ -274,9 +356,10 @@
             dma((4,)),
             dma((n_e,)),
             dma((n_e,)),
-            dma((chunks, n_z)),
+            dma((n_e,)),
+            dma((n_e,)),
+            dma((chunks, 2 * n_z)),
             dma((chunks, n_e)),
-            dma((chunks, n_z)),
             dma((chunks, n_dp)),
             dma((chunks, n_dp)),
             dma((chunks, n_dp)),
@@ -293,7 +376,7 @@
             transcendentals=rows * hidden,
         ),
     )(routes.T, gates.T, latent, up_proj, expert_in, expert_out, cotangent)
-    return mixed, grad.reshape(width, features).astype(jnp.float32)
+    return finish(mixed, grad.reshape(width, features))
 
 
 def solution(mesh):

time: 41.7 us -> 72.5 us (1.74)
  Pallas kernels: 36.4 us -> 71.7 us
  local copies, waits for them, and re-layouts: 2.26 us -> 0 us
  other arithmetic: 2.15 us -> 0 us
    pallas_call x0 -> x1, Pallas kernels: none -> 33 us  [finish(): pl.pallas_call(functools.partial(finish_kernel, parts), out_shape=(jax.Sh...]
    pallas_call x1, Pallas kernels: 36.4 us -> 38.7 us  [body(): pl.pallas_call(functools.partial(kernel, n_e, n_dp, chunks), out_shape=(j...]
    unnamed x1 -> x0, local copies, waits for them, and re-layouts: 2.26 us -> none
    convert_element_type x1 -> x0, other arithmetic: 2.15 us -> none  [body(): return (mixed, grad.reshape(width, features).astype(jnp.float32))]
where the time goes in v2:
time: 72.5 us; the launch traced here: 72.3 us
  Pallas kernels  71.7 us (99%)
    pallas_call x1, Pallas kernels, body(): pl.pallas_call(functools.partial(kernel, n_e, n_dp, chunks), out_shape=(j...  38.7 us
    pallas_call x1, Pallas kernels, finish(): pl.pallas_call(functools.partial(finish_kernel, parts), out_shape=(jax.Sh...  33 us

profile of v2, /device:TPU:0, one launch (start us, length us, event | category | flops | bytes accessed | tf_op | source)
XLA Modules:
  0.0 72.3 jit_solution(17766406276945293875)
XLA Ops:
  0.6 38.7 %shard_map.86 = (bf16[1024,512]{1,0:T(8,128)(2,1)}, bf16[4,4,32,512]{3,2,1,0:T(8,128)(2,1)}) custom-call(s32[8,128]{1,0:T(8,128)} %bitcast.4, bf16[8,128]{1,0:T(8,128)(2,1)} %bitcast.5, bf16[128,512]{1,0:T(8,128)(2,1)} %latent_ref.1, bf16[512,512]{1,0:T(8,128)(2,1)} %up_hbm.1, bf16[1,512,4096]{2,1,0:T(8,128)(2,1)} %win_hbm.1, ...), custom_call_target="tpu_custom_call" | custom-call | flops 1879048192 | bytes 10485760 | tf_op jit(solution)/shard_map/pallas_call | solution.py:330
  39.4 33.0 %shard_map.87 = (bf16[1024,512]{1,0:T(8,128)(2,1)}, f32[512,512]{1,0:T(8,128)}) custom-call(bf16[1024,512]{1,0:T(8,128)(2,1)} %get-tuple-element.4.mixed_ref, bf16[512,512]{1,0:T(8,128)(2,1)} %bitcast.3), custom_call_target="tpu_custom_call" | custom-call | tf_op jit(solution)/shard_map/pallas_call | solution.py:298

commit v3 on v1

--- a/solution.py
+++ b/solution.py
@@ -233,11 +233,69 @@
     out.wait()
 
 
+def finish_kernel(parts, mixed_ref, grad_ref, mixed_out, grad_out, held, narrow, wide, in_sem, out_sem):
+    tall, deep = mixed_ref.shape[0] // parts, grad_ref.shape[0] // parts
+    ins, outs = [], []
+    for i in range(parts):
+        low = pltpu.make_async_copy(
+            grad_ref.at[pl.ds(i * deep, deep)], narrow.at[i], in_sem.at[0, i]
+        )
+        low.start()
+        row = pltpu.make_async_copy(
+            mixed_ref.at[pl.ds(i * tall, tall)], held.at[i], in_sem.at[1, i]
+        )
+        row.start()
+        ins.append((low, row))
+    for i in range(parts):
+        low, row = ins[i]
+        low.wait()
+        wide[i] = narrow[i].astype(jnp.float32)
+        outs.append(
+            pltpu.make_async_copy(
+                wide.at[i], grad_out.at[pl.ds(i * deep, deep)], out_sem.at[0, i]
+            )
+        )
+        outs[-1].start()
+        row.wait()
+        outs.append(
+            pltpu.make_async_copy(
+                held.at[i], mixed_out.at[pl.ds(i * tall, tall)], out_sem.at[1, i]
+            )
+        )
+        outs[-1].start()
+    for copy in outs:
+        copy.wait()
+
+
+def finish(mixed, grad):
+    parts = 4
+    deep, features = grad.shape[0] // parts, grad.shape[1]
+    hbm = pl.BlockSpec(memory_space=pl.ANY)
+    dma = pltpu.SemaphoreType.DMA
+    return pl.pallas_call(
+        functools.partial(finish_kernel, parts),
+        out_shape=(
+            jax.ShapeDtypeStruct(mixed.shape, mixed.dtype),
+            jax.ShapeDtypeStruct(grad.shape, jnp.float32),
+        ),
+        in_specs=[hbm, hbm],
+        out_specs=(hbm, hbm),
+        scratch_shapes=[
+            pltpu.VMEM((parts, mixed.shape[0] // parts, features), jnp.bfloat16),
+            pltpu.VMEM((parts, deep, features), jnp.bfloat16),
+            pltpu.VMEM((parts, deep, features), jnp.float32),
+            dma((2, parts)),
+            dma((2, parts)),
+        ],
+        compiler_params=pltpu.CompilerParams(vmem_limit_bytes=56 * 1024 * 1024),
+    )(mixed, grad)
+
+
 def body(n_e, n_dp, latent, up_proj, expert_in, expert_out, routes, gates, cotangent):
     tok, width = latent.shape
     hidden = expert_out.shape[1]
     group, features = cotangent.shape
-    chunks = max(1, min(4, width // (16 * n_dp)))
+    chunks = max(1, min(2, width // (16 * n_dp)))
     cols = width // chunks
     share = cols // n_dp
     rows = n_e * SLOTS
@@ -293,7 +351,7 @@
             transcendentals=rows * hidden,
         ),
     )(routes.T, gates.T, latent, up_proj, expert_in, expert_out, cotangent)
-    return mixed, grad.reshape(width, features).astype(jnp.float32)
+    return finish(mixed, grad.reshape(width, features))
 
 
 def solution(mesh):

time: 41.7 us -> 40.5 us (0.971)
  Pallas kernels: 36.4 us -> 39.7 us
  local copies, waits for them, and re-layouts: 2.26 us -> 0 us
  other arithmetic: 2.15 us -> 0 us
    pallas_call x0 -> x1, Pallas kernels: none -> 2.38 us  [finish(): pl.pallas_call(functools.partial(finish_kernel, parts), out_shape=(jax.Sh...]
    unnamed x1 -> x0, local copies, waits for them, and re-layouts: 2.26 us -> none
    convert_element_type x1 -> x0, other arithmetic: 2.15 us -> none  [body(): return (mixed, grad.reshape(width, features).astype(jnp.float32))]
    pallas_call x1, Pallas kernels: 36.4 us -> 37.3 us  [body(): pl.pallas_call(functools.partial(kernel, n_e, n_dp, chunks), out_shape=(j...]
where the time goes in v3:
time: 40.5 us; the launch traced here: 40.3 us
  Pallas kernels  39.7 us (98%)
  between operations  0.64 us (2%)
    pallas_call x1, Pallas kernels, body(): pl.pallas_call(functools.partial(kernel, n_e, n_dp, chunks), out_shape=(j...  37.3 us
    pallas_call x1, Pallas kernels, finish(): pl.pallas_call(functools.partial(finish_kernel, parts), out_shape=(jax.Sh...  2.38 us

profile of v3, /device:TPU:0, one launch (start us, length us, event | category | flops | bytes accessed | tf_op | source)
XLA Modules:
  0.0 40.3 jit_solution(6801564729207853618)
XLA Ops:
  0.6 37.3 %shard_map.86 = (bf16[1024,512]{1,0:T(8,128)(2,1)}, bf16[2,4,64,512]{3,2,1,0:T(8,128)(2,1)}) custom-call(s32[8,128]{1,0:T(8,128)} %bitcast.4, bf16[8,128]{1,0:T(8,128)(2,1)} %bitcast.5, bf16[128,512]{1,0:T(8,128)(2,1)} %latent_ref.1, bf16[512,512]{1,0:T(8,128)(2,1)} %up_hbm.1, bf16[1,512,4096]{2,1,0:T(8,128)(2,1)} %win_hbm.1, ...), custom_call_target="tpu_custom_call" | custom-call | flops 1879048192 | bytes 10485760 | tf_op jit(solution)/shard_map/pallas_call | solution.py:308
  37.9 2.4 %shard_map.87 = (bf16[1024,512]{1,0:T(8,128)(2,1)}, f32[512,512]{1,0:T(8,128)}) custom-call(bf16[1024,512]{1,0:T(8,128)(2,1)} %get-tuple-element.4.mixed_ref, bf16[512,512]{1,0:T(8,128)(2,1)} %bitcast.3), custom_call_target="tpu_custom_call" | custom-call | tf_op jit(solution)/shard_map/pallas_call | solution.py:275

commit v4 on v2

--- a/solution.py
+++ b/solution.py
@@ -138,11 +138,14 @@
         copy.start()
         sends.append(copy)
 
-    relay = n_z == 4
     near = (z + 1 - 2 * lax.rem(z, 2)) * CORES + core
     over = lax.rem(z + 2, n_z) * CORES + core
     far = (n_z - 1 - z) * CORES + core
-    direct = [over, near] if relay else z_peers
+    relayed = [n_z == 4 and 0 < c < chunks - 1 for c in range(chunks)]
+    every = [over, far, near] if n_z == 4 else z_peers
+
+    def direct(c):
+        return [over, near] if relayed[c] else every
 
     loads[1].wait()
     for c in range(chunks):
@@ -150,22 +153,22 @@
             act[...], wout[:, c * cols : (c + 1) * cols], preferred_element_type=jnp.float32
         ).astype(jnp.bfloat16)
         rsend[c] = result
-        for i, peer in enumerate(direct + [sibling]):
+        for i, peer in enumerate(direct(c) + [sibling]):
             send(c, me, peer, i, rsend.at[c])
         gbuf[c, me] = result
 
     def first(c):
-        sem = len(direct) + 1
-        for peer in direct:
+        sem = len(direct(c)) + 1
+        for peer in direct(c):
             landed(c, peer)
-            if relay and peer is over:
+            if relayed[c] and peer is over:
                 send(c, peer, near, sem, gbuf.at[c, peer])
                 sem += 1
             send(c, peer, sibling, sem, gbuf.at[c, peer])
             sem += 1
 
     def second(c):
-        if relay:
+        if relayed[c]:
             landed(c, far)
             send(c, far, sibling, 2 * n_z - 2, gbuf.at[c, far])
         landed(c, sibling)
@@ -215,10 +218,12 @@
             spread_sum(c, dp, peer).start()
         own_sum(c).start()
 
-    first(0)
     for c in range(chunks):
-        if c + 1 < chunks:
-            first(c + 1)
+        if not relayed[c]:
+            first(c)
+        elif not relayed[c - 1]:
+            for later in range(c, chunks - 1):
+                first(later)
         second(c)
 
         def combine(b):
@@ -266,27 +271,37 @@
     out.wait()
 
 
-def finish_kernel(parts, mixed_ref, grad_ref, mixed_out, grad_out, narrow, wide, copy_sem, in_sem, out_sem):
+def finish_kernel(parts, mixed_ref, grad_ref, mixed_out, grad_out, held, narrow, wide, in_sem, out_sem):
     tall, deep = mixed_ref.shape[0] // parts, grad_ref.shape[0] // parts
-    copies, outs = [], []
-    ins = [
-        pltpu.make_async_copy(grad_ref.at[pl.ds(i * deep, deep)], narrow.at[i], in_sem.at[i])
-        for i in range(parts)
-    ]
-    for load in ins:
-        load.start()
+    ins, outs = [], []
     for i in range(parts):
-        at = pl.ds(i * tall, tall)
-        copies.append(pltpu.make_async_copy(mixed_ref.at[at], mixed_out.at[at], copy_sem.at[i]))
-        copies[-1].start()
+        low = pltpu.make_async_copy(
+            grad_ref.at[pl.ds(i * deep, deep)], narrow.at[i], in_sem.at[0, i]
+        )
+        low.start()
+        row = pltpu.make_async_copy(
+            mixed_ref.at[pl.ds(i * tall, tall)], held.at[i], in_sem.at[1, i]
+        )
+        row.start()
+        ins.append((low, row))
     for i in range(parts):
-        ins[i].wait()
+        low, row = ins[i]
+        low.wait()
         wide[i] = narrow[i].astype(jnp.float32)
         outs.append(
-            pltpu.make_async_copy(wide.at[i], grad_out.at[pl.ds(i * deep, deep)], out_sem.at[i])
+            pltpu.make_async_copy(
+                wide.at[i], grad_out.at[pl.ds(i * deep, deep)], out_sem.at[0, i]
+            )
         )
         outs[-1].start()
-    for copy in copies + outs:
+        row.wait()
+        outs.append(
+            pltpu.make_async_copy(
+                held.at[i], mixed_out.at[pl.ds(i * tall, tall)], out_sem.at[1, i]
+            )
+        )
+        outs[-1].start()
+    for copy in outs:
         copy.wait()
 
 
@@ -304,11 +319,11 @@
         in_specs=[hbm, hbm],
         out_specs=(hbm, hbm),
         scratch_shapes=[
+            pltpu.VMEM((parts, mixed.shape[0] // parts, features), jnp.bfloat16),
             pltpu.VMEM((parts, deep, features), jnp.bfloat16),
             pltpu.VMEM((parts, deep, features), jnp.float32),
-            dma((parts,)),
-            dma((parts,)),
-            dma((parts,)),
+            dma((2, parts)),
+            dma((2, parts)),
         ],
         compiler_params=pltpu.CompilerParams(vmem_limit_bytes=56 * 1024 * 1024),
     )(mixed, grad)

time: 72.5 us -> 41.8 us (0.58)
  Pallas kernels: 71.7 us -> 41 us
    pallas_call x1, Pallas kernels: 33 us -> 2.38 us  [finish(): pl.pallas_call(functools.partial(finish_kernel, parts), out_shape=(jax.Sh...]
where the time goes in v4:
time: 41.8 us; the launch traced here: 41.6 us
  Pallas kernels  41 us (98%)
  between operations  0.64 us (2%)
    pallas_call x1, Pallas kernels, body(): pl.pallas_call(functools.partial(kernel, n_e, n_dp, chunks), out_shape=(j...  38.6 us
    pallas_call x1, Pallas kernels, finish(): pl.pallas_call(functools.partial(finish_kernel, parts), out_shape=(jax.Sh...  2.38 us

profile of v4, /device:TPU:0, one launch (start us, length us, event | category | flops | bytes accessed | tf_op | source)
XLA Modules:
  0.0 41.6 jit_solution(6909915443531750216)
XLA Ops:
  0.6 38.6 %shard_map.86 = (bf16[1024,512]{1,0:T(8,128)(2,1)}, bf16[4,4,32,512]{3,2,1,0:T(8,128)(2,1)}) custom-call(s32[8,128]{1,0:T(8,128)} %bitcast.4, bf16[8,128]{1,0:T(8,128)(2,1)} %bitcast.5, bf16[128,512]{1,0:T(8,128)(2,1)} %latent_ref.1, bf16[512,512]{1,0:T(8,128)(2,1)} %up_hbm.1, bf16[1,512,4096]{2,1,0:T(8,128)(2,1)} %win_hbm.1, ...), custom_call_target="tpu_custom_call" | custom-call | flops 1879048192 | bytes 10485760 | tf_op jit(solution)/shard_map/pallas_call | solution.py:345
  39.3 2.4 %shard_map.87 = (bf16[1024,512]{1,0:T(8,128)(2,1)}, f32[512,512]{1,0:T(8,128)}) custom-call(bf16[1024,512]{1,0:T(8,128)(2,1)} %get-tuple-element.4.mixed_ref, bf16[512,512]{1,0:T(8,128)(2,1)} %bitcast.3), custom_call_target="tpu_custom_call" | custom-call | tf_op jit(solution)/shard_map/pallas_call | solution.py:313

commit v5 on v3

--- a/solution.py
+++ b/solution.py
@@ -9,7 +9,12 @@
 
 MESH = pl.DeviceIdType.MESH
 SLOTS = 16
+CAP = 13
 CORES = 2
+
+
+def message_rows(n_e, tok, width):
+    return -(-(CAP + n_e * tok // width) // SLOTS) * SLOTS
 
 
 def each(count, step):
@@ -59,7 +64,8 @@
     rows = n_e * SLOTS
     cols = width // chunks
     share = cols // n_dp
-    meta_parts = (2 * n_e) // SLOTS
+    tall = dsend.shape[1]
+    per_row = width // tok
 
     expert_of = lax.broadcasted_iota(jnp.int32, (n_e, tok), 0)
     named = jnp.zeros((n_e, tok), jnp.float32)
@@ -71,24 +77,27 @@
     earlier = lax.broadcasted_iota(jnp.int32, (tok, tok), 0) < lax.broadcasted_iota(
         jnp.int32, (tok, tok), 1
     )
-    before = jnp.dot(
-        named.astype(jnp.bfloat16),
-        jnp.where(earlier, 1.0, 0.0).astype(jnp.bfloat16),
-        preferred_element_type=jnp.float32,
-    )
+    ahead = jnp.where(earlier, 1.0, 0.0).astype(jnp.bfloat16)
+    before = jnp.dot(named.astype(jnp.bfloat16), ahead, preferred_element_type=jnp.float32)
     slot = jnp.where(named > 0.0, before, -1.0)
     slot_of = lax.broadcasted_iota(jnp.int32, (SLOTS, tok), 0).astype(jnp.float32)
     pick = jnp.concatenate(
         [jnp.where(slot[e : e + 1, :] == slot_of, 1.0, 0.0) for e in range(n_e)], axis=0
     ).astype(jnp.bfloat16)
     outgoing = jnp.dot(pick, latent_ref[...], preferred_element_type=jnp.float32)
-    dsend[:, :, :width] = outgoing.astype(jnp.bfloat16).reshape(n_e, SLOTS, width)
-    meta = jnp.concatenate([slot, gate], axis=0).astype(jnp.bfloat16)
-    for j in range(meta_parts):
-        part = meta[j * SLOTS : (j + 1) * SLOTS, :]
-        dsend[:, :, width + j * tok : width + (j + 1) * tok] = jnp.broadcast_to(
-            part[None], (n_e, SLOTS, tok)
-        )
+    outgoing = outgoing.reshape(n_e, SLOTS, width)
+    if tall > SLOTS:
+        outgoing = jnp.concatenate(
+            [outgoing, jnp.zeros((n_e, tall - SLOTS, width), jnp.float32)], axis=1
+        )
+    row_of = lax.broadcasted_iota(jnp.int32, (tall, width), 0)
+    extra = jnp.zeros((tall, width), jnp.float32)
+    for i in range(n_e // per_row):
+        line = jnp.concatenate(
+            [gate[e : e + 1, :] for e in range(i * per_row, (i + 1) * per_row)], axis=1
+        )
+        extra = jnp.where(row_of == CAP + i, line, extra)
+    dsend[...] = (outgoing + extra[None]).astype(jnp.bfloat16)
     drecv[me] = dsend[me]
 
     pl.semaphore_wait(barrier, n_e - 1 + n_dp - 1)
@@ -106,7 +115,7 @@
     for peer in e_peers:
         dispatch(peer, peer).wait_recv()
 
-    arrived = drecv[:, :, :width].reshape(rows, width)
+    arrived = drecv[:, :SLOTS, :].reshape(rows, width)
     tile = min(512, hidden)
     for j in range(hidden // tile):
         g = jnp.dot(arrived, win[:, j * tile : (j + 1) * tile], preferred_element_type=jnp.float32)
@@ -137,12 +146,22 @@
         gbuf[c, me] = result
 
     def weigh(b):
-        both = jnp.concatenate(
-            [drecv[b, :, width + j * tok : width + (j + 1) * tok] for j in range(meta_parts)], axis=0
-        ).astype(jnp.float32)
+        sent = drecv[b].astype(jnp.float32)
+        theirs = jnp.concatenate(
+            [
+                sent[CAP + e // per_row : CAP + e // per_row + 1, e % per_row * tok : (e % per_row + 1) * tok]
+                for e in range(n_e)
+            ],
+            axis=0,
+        )
+        live = theirs > 0.0
+        count = jnp.dot(
+            jnp.where(live, 1.0, 0.0).astype(jnp.bfloat16), ahead, preferred_element_type=jnp.float32
+        )
+        place = jnp.where(live, count, -1.0)
         spread = jnp.concatenate(
             [
-                jnp.where(both[e : e + 1, :] == slot_of, both[n_e + e : n_e + e + 1, :], 0.0)
+                jnp.where(place[e : e + 1, :] == slot_of, theirs[e : e + 1, :], 0.0)
                 for e in range(n_e)
             ],
             axis=0,
@@ -295,12 +314,12 @@
     tok, width = latent.shape
     hidden = expert_out.shape[1]
     group, features = cotangent.shape
-    chunks = max(1, min(2, width // (16 * n_dp)))
+    chunks = max(1, min(4, width // (16 * n_dp)))
     cols = width // chunks
     share = cols // n_dp
     rows = n_e * SLOTS
     n_z = n_e // CORES
-    wide = width + (2 * n_e // SLOTS) * tok
+    tall = message_rows(n_e, tok, width)
     vmem = pl.BlockSpec(memory_space=pltpu.VMEM)
     hbm = pl.BlockSpec(memory_space=pl.ANY)
     bf16 = jnp.bfloat16
@@ -318,8 +337,8 @@
             pltpu.VMEM((hidden, width), bf16),
             pltpu.VMEM((group, features), bf16),
             pltpu.VMEM((width, features), bf16),
-            pltpu.VMEM((n_e, SLOTS, wide), bf16),
-            pltpu.VMEM((n_e, SLOTS, wide), bf16),
+            pltpu.VMEM((n_e, tall, width), bf16),
+            pltpu.VMEM((n_e, tall, width), bf16),
             pltpu.VMEM((rows, hidden), bf16),
             pltpu.VMEM((chunks, rows, cols), bf16),
             pltpu.VMEM((chunks, n_e, rows, cols), bf16),

time: 40.5 us -> 39.3 us (0.970)
  Pallas kernels: 39.7 us -> 38.5 us
    pallas_call x1, Pallas kernels: 37.3 us -> 36.1 us  [body(): pl.pallas_call(functools.partial(kernel, n_e, n_dp, chunks), out_shape=(j...]
where the time goes in v5:
time: 39.3 us; the launch traced here: 39.2 us
  Pallas kernels  38.5 us (98%)
  between operations  0.64 us (2%)
    pallas_call x1, Pallas kernels, body(): pl.pallas_call(functools.partial(kernel, n_e, n_dp, chunks), out_shape=(j...  36.1 us
    pallas_call x1, Pallas kernels, finish(): pl.pallas_call(functools.partial(finish_kernel, parts), out_shape=(jax.Sh...  2.38 us

profile of v5, /device:TPU:0, one launch (start us, length us, event | category | flops | bytes accessed | tf_op | source)
XLA Modules:
  0.0 39.2 jit_solution(7712878354767050395)
XLA Ops:
  0.6 36.1 %shard_map.86 = (bf16[1024,512]{1,0:T(8,128)(2,1)}, bf16[4,4,32,512]{3,2,1,0:T(8,128)(2,1)}) custom-call(s32[8,128]{1,0:T(8,128)} %bitcast.4, bf16[8,128]{1,0:T(8,128)(2,1)} %bitcast.5, bf16[128,512]{1,0:T(8,128)(2,1)} %latent_ref.1, bf16[512,512]{1,0:T(8,128)(2,1)} %up_hbm.1, bf16[1,512,4096]{2,1,0:T(8,128)(2,1)} %win_hbm.1, ...), custom_call_target="tpu_custom_call" | custom-call | flops 1879048192 | bytes 10485760 | tf_op jit(solution)/shard_map/pallas_call | solution.py:327
  36.8 2.4 %shard_map.87 = (bf16[1024,512]{1,0:T(8,128)(2,1)}, f32[512,512]{1,0:T(8,128)}) custom-call(bf16[1024,512]{1,0:T(8,128)(2,1)} %get-tuple-element.4.mixed_ref, bf16[512,512]{1,0:T(8,128)(2,1)} %bitcast.3), custom_call_target="tpu_custom_call" | custom-call | tf_op jit(solution)/shard_map/pallas_call | solution.py:294

commit v6 on v5

--- a/solution.py
+++ b/solution.py
@@ -28,9 +28,9 @@
 def kernel(
     n_e, n_dp, chunks,
     routes_ref, gates_ref, latent_ref, up_hbm, win_hbm, wout_hbm, cot_hbm,
-    mixed_hbm, grad_hbm,
-    win, wout, cot, up, dsend, drecv, act, rsend, gbuf, weight, comb, mixed, gsend, rsbuf, asend,
-    load_sem, d_send, d_recv, g_send, g_recv, f_send, r_send, r_recv, a_send, a_recv, own_sem, out_sem,
+    mixed, grad,
+    win, wout, cot, up, dsend, drecv, act, rsend, gbuf, weight, comb, gsend, rsbuf, asend,
+    load_sem, d_send, d_recv, g_send, g_recv, f_send, r_send, r_recv, a_send, a_recv,
 ):
     me = lax.axis_index("expert")
     dp = lax.axis_index("dp")
@@ -180,13 +180,10 @@
 
     def spread_sum(c, slot_, peer):
         return pltpu.make_async_remote_copy(
-            src_ref=asend.at[c], dst_ref=grad_hbm.at[c, slot_],
+            src_ref=asend.at[c], dst_ref=grad.at[c, slot_],
             send_sem=a_send.at[c, peer], recv_sem=a_recv.at[c, slot_],
             device_id={"dp": peer}, device_id_type=MESH,
         )
-
-    def own_sum(c):
-        return pltpu.make_async_copy(asend.at[c], grad_hbm.at[c, dp], own_sem.at[c])
 
     def reduce(c):
         total = gsend[c, dp].astype(jnp.float32)
@@ -196,7 +193,7 @@
         asend[c] = total.astype(jnp.bfloat16)
         for peer in dp_peers:
             spread_sum(c, dp, peer).start()
-        own_sum(c).start()
+        grad[c, dp] = asend[c]
 
     for c in range(chunks):
         for i, peer in enumerate(z_peers):
@@ -234,10 +231,10 @@
             comb[at, :], up[...], preferred_element_type=jnp.float32
         ).astype(jnp.bfloat16)
 
-    each(n_e, project)
-    out = pltpu.make_async_copy(mixed, mixed_hbm, out_sem)
-    out.start()
+    half = n_e // 2
+    each(half, project)
     reduce(chunks - 1)
+    each(n_e - half, lambda b: project(half + b))
 
     for peer in e_peers:
         dispatch(me, peer).wait_send()
@@ -248,65 +245,42 @@
             scatter(c, dp, peer).wait_send()
             spread_sum(c, dp, peer).wait_send()
             spread_sum(c, peer, peer).wait_recv()
-        own_sum(c).wait()
-    out.wait()
-
-
-def finish_kernel(parts, mixed_ref, grad_ref, mixed_out, grad_out, held, narrow, wide, in_sem, out_sem):
-    tall, deep = mixed_ref.shape[0] // parts, grad_ref.shape[0] // parts
-    ins, outs = [], []
-    for i in range(parts):
-        low = pltpu.make_async_copy(
-            grad_ref.at[pl.ds(i * deep, deep)], narrow.at[i], in_sem.at[0, i]
-        )
-        low.start()
-        row = pltpu.make_async_copy(
-            mixed_ref.at[pl.ds(i * tall, tall)], held.at[i], in_sem.at[1, i]
-        )
-        row.start()
-        ins.append((low, row))
-    for i in range(parts):
-        low, row = ins[i]
-        low.wait()
-        wide[i] = narrow[i].astype(jnp.float32)
-        outs.append(
-            pltpu.make_async_copy(
-                wide.at[i], grad_out.at[pl.ds(i * deep, deep)], out_sem.at[0, i]
-            )
-        )
+
+
+def finish_kernel(mixed_ref, grad_ref, mixed_out, grad_out, wide, mixed_sem, grad_sem):
+    copy = pltpu.make_async_copy(mixed_ref, mixed_out, mixed_sem)
+    copy.start()
+    chunks, n_dp, share = grad_ref.shape[:3]
+    outs = []
+    for c in range(chunks):
+        wide[c] = grad_ref[c].astype(jnp.float32).reshape(n_dp * share, grad_ref.shape[3])
+        at = pl.ds(c * n_dp * share, n_dp * share)
+        outs.append(pltpu.make_async_copy(wide.at[c], grad_out.at[at], grad_sem.at[c]))
         outs[-1].start()
-        row.wait()
-        outs.append(
-            pltpu.make_async_copy(
-                held.at[i], mixed_out.at[pl.ds(i * tall, tall)], out_sem.at[1, i]
-            )
-        )
-        outs[-1].start()
-    for copy in outs:
-        copy.wait()
+    copy.wait()
+    for out in outs:
+        out.wait()
 
 
 def finish(mixed, grad):
-    parts = 4
-    deep, features = grad.shape[0] // parts, grad.shape[1]
+    chunks, n_dp, share, features = grad.shape
+    vmem = pl.BlockSpec(memory_space=pltpu.VMEM)
     hbm = pl.BlockSpec(memory_space=pl.ANY)
     dma = pltpu.SemaphoreType.DMA
     return pl.pallas_call(
-        functools.partial(finish_kernel, parts),
+        finish_kernel,
         out_shape=(
             jax.ShapeDtypeStruct(mixed.shape, mixed.dtype),
-            jax.ShapeDtypeStruct(grad.shape, jnp.float32),
+            jax.ShapeDtypeStruct((chunks * n_dp * share, features), jnp.float32),
         ),
-        in_specs=[hbm, hbm],
+        in_specs=[vmem, vmem],
         out_specs=(hbm, hbm),
         scratch_shapes=[
-            pltpu.VMEM((parts, mixed.shape[0] // parts, features), jnp.bfloat16),
-            pltpu.VMEM((parts, deep, features), jnp.bfloat16),
-            pltpu.VMEM((parts, deep, features), jnp.float32),
-            dma((2, parts)),
-            dma((2, parts)),
+            pltpu.VMEM((chunks, n_dp * share, features), jnp.float32),
+            dma,
+            dma((chunks,)),
         ],
-        compiler_params=pltpu.CompilerParams(vmem_limit_bytes=56 * 1024 * 1024),
+        compiler_params=pltpu.CompilerParams(vmem_limit_bytes=50 * 1024 * 1024),
     )(mixed, grad)
 
 
@@ -327,11 +301,11 @@
     mixed, grad = pl.pallas_call(
         functools.partial(kernel, n_e, n_dp, chunks),
         out_shape=(
-            jax.ShapeDtypeStruct((group, features), bf16),
-            jax.ShapeDtypeStruct((chunks, n_dp, share, features), bf16),
+            pltpu.VMEM((group, features), bf16),
+            pltpu.VMEM((chunks, n_dp, share, features), bf16),
         ),
         in_specs=[vmem, vmem, vmem, hbm, hbm, hbm, hbm],
-        out_specs=(hbm, hbm),
+        out_specs=(vmem, vmem),
         scratch_shapes=[
             pltpu.VMEM((width, 2 * hidden), bf16),
             pltpu.VMEM((hidden, width), bf16),
@@ -344,7 +318,6 @@
             pltpu.VMEM((chunks, n_e, rows, cols), bf16),
             pltpu.VMEM((n_e, tok, rows), bf16),
             pltpu.VMEM((group, width), bf16),
-            pltpu.VMEM((group, features), bf16),
             pltpu.VMEM((chunks, n_dp, share, features), bf16),
             pltpu.VMEM((chunks, n_dp, share, features), bf16),
             pltpu.VMEM((chunks, share, features), bf16),
@@ -358,11 +331,9 @@
             dma((chunks, n_dp)),
             dma((chunks, n_dp)),
             dma((chunks, n_dp)),
-            dma((chunks,)),
-            dma,
         ],
         compiler_params=pltpu.CompilerParams(
-            collective_id=0, has_side_effects=True, vmem_limit_bytes=56 * 1024 * 1024
+            collective_id=0, has_side_effects=True, vmem_limit_bytes=54 * 1024 * 1024
         ),
         cost_estimate=pl.CostEstimate(
             flops=2 * rows * width * hidden * 3 + 4 * group * width * features,
@@ -370,7 +341,7 @@
             transcendentals=rows * hidden,
         ),
     )(routes.T, gates.T, latent, up_proj, expert_in, expert_out, cotangent)
-    return finish(mixed, grad.reshape(width, features))
+    return finish(mixed, grad)
 
 
 def solution(mesh):

time: 39.3 us -> 38.1 us (0.969)
  Pallas kernels: 38.5 us -> 37.3 us
    pallas_call x2, Pallas kernels: 38.5 us -> 37.3 us  [the longest x1 35.9 us: body(): pl.pallas_call(functools.partial(kernel, n_e, n_dp, chunks), out_shape=(p...]
where the time goes in v6:
time: 38.1 us; the launch traced here: 37.9 us
  Pallas kernels  37.3 us (98%)
  between operations  0.64 us (2%)
    pallas_call x1, Pallas kernels, body(): pl.pallas_call(functools.partial(kernel, n_e, n_dp, chunks), out_shape=(p...  35.9 us
    pallas_call x1, Pallas kernels, finish(): pl.pallas_call(finish_kernel, out_shape=(jax.ShapeDtypeStruct(mixed.shape...  1.35 us

profile of v6, /device:TPU:0, one launch (start us, length us, event | category | flops | bytes accessed | tf_op | source)
XLA Modules:
  0.0 37.9 jit_solution(6592131333261332803)
XLA Ops:
  0.6 35.9 %shard_map.86 = (bf16[1024,512]{1,0:T(8,128)(2,1)S(1)}, bf16[4,4,32,512]{3,2,1,0:T(8,128)(2,1)S(1)}) custom-call(s32[8,128]{1,0:T(8,128)} %bitcast.2, bf16[8,128]{1,0:T(8,128)(2,1)} %bitcast.3, bf16[128,512]{1,0:T(8,128)(2,1)} %latent_ref.1, bf16[512,512]{1,0:T(8,128)(2,1)} %up_hbm.1, bf16[1,512,4096]{2,1,0:T(8,128)(2,1)} %win_hbm.1, ...), custom_call_target="tpu_custom_call" | custom-call | flops 1879048192 | bytes 10485760 | tf_op jit(solution)/shard_map/pallas_call | solution.py:301
  36.6 1.4 %shard_map.87 = (bf16[1024,512]{1,0:T(8,128)(2,1)}, f32[512,512]{1,0:T(8,128)}) custom-call(bf16[1024,512]{1,0:T(8,128)(2,1)S(1)} %get-tuple-element.4.mixed_ref, bf16[4,4,32,512]{3,2,1,0:T(8,128)(2,1)S(1)} %get-tuple-element.5.grad_ref), custom_call_target="tpu_custom_call" | custom-call | tf_op jit(solution)/shard_map/pallas_call | solution.py:270

commit v7 on v6

--- a/solution.py
+++ b/solution.py
@@ -26,7 +26,7 @@
 
 
 def kernel(
-    n_e, n_dp, chunks,
+    n_e, n_dp, units, plan,
     routes_ref, gates_ref, latent_ref, up_hbm, win_hbm, wout_hbm, cot_hbm,
     mixed, grad,
     win, wout, cot, up, dsend, drecv, act, rsend, gbuf, weight, comb, gsend, rsbuf, asend,
@@ -37,8 +37,12 @@
     n_z = n_e // CORES
     z, core = me // CORES, lax.rem(me, CORES)
     sibling = z * CORES + (CORES - 1 - core)
-    z_peers = [lax.rem(z + off, n_z) * CORES + core for off in range(1, n_z)]
-    f_peers = [lax.rem(z + off, n_z) * CORES + (CORES - 1 - core) for off in range(1, n_z)]
+    if n_z == 4:
+        others = [z + 1 - 2 * lax.rem(z, 2), lax.rem(z + 2, n_z), n_z - 1 - z]
+    else:
+        others = [lax.rem(z + off, n_z) for off in range(1, n_z)]
+    z_peers = [other * CORES + core for other in others]
+    f_peers = [other * CORES + (CORES - 1 - core) for other in others]
     e_peers = [lax.rem(me + off, n_e) for off in range(1, n_e)]
     dp_peers = [lax.rem(dp + off, n_dp) for off in range(1, n_dp)]
 
@@ -62,8 +66,8 @@
     hidden = wout.shape[0]
     top = routes_ref.shape[0]
     rows = n_e * SLOTS
-    cols = width // chunks
-    share = cols // n_dp
+    cols = width // units
+    chunks = len(plan)
     tall = dsend.shape[1]
     per_row = width // tok
 
@@ -125,25 +129,31 @@
         )
         act[:, j * tile : (j + 1) * tile] = (g / (1.0 + jnp.exp(-g)) * u).astype(jnp.bfloat16)
 
+    def held(c, source):
+        return gbuf.at[pl.ds(*plan[c]), source]
+
     def gather(c, source, peer, peer_slot, src, sems):
         return pltpu.make_async_remote_copy(
-            src_ref=src, dst_ref=gbuf.at[c, source],
+            src_ref=src, dst_ref=held(c, source),
             send_sem=sems.at[c, peer_slot], recv_sem=g_recv.at[c, source],
             device_id={"expert": peer}, device_id_type=MESH,
         )
 
     loads[1].wait()
     sends = []
-    for c in range(chunks):
+    for c, (start, count) in enumerate(plan):
         result = jnp.dot(
-            act[...], wout[:, c * cols : (c + 1) * cols], preferred_element_type=jnp.float32
+            act[...], wout[:, start * cols : (start + count) * cols],
+            preferred_element_type=jnp.float32,
         ).astype(jnp.bfloat16)
-        rsend[c] = result
-        for i, peer in enumerate(z_peers + [sibling]):
-            copy = gather(c, me, peer, i, rsend.at[c], g_send)
+        for u in range(count):
+            rsend[start + u] = result[:, u * cols : (u + 1) * cols]
+        for i, peer in enumerate(z_peers[::-1] + [sibling]):
+            copy = gather(c, me, peer, i, rsend.at[pl.ds(start, count)], g_send)
             copy.start()
             sends.append(copy)
-        gbuf[c, me] = result
+        for u in range(count):
+            gbuf[start + u, me] = result[:, u * cols : (u + 1) * cols]
 
     def weigh(b):
         sent = drecv[b].astype(jnp.float32)
@@ -171,53 +181,70 @@
     each(n_e, weigh)
     loads[2].wait()
 
+    def rows_of(c, owner):
+        start, count = plan[c]
+        share = count * cols // n_dp
+        return pl.ds(start * cols + owner * share, share)
+
+    def sum_rows(c):
+        start, count = plan[c]
+        return pl.ds(start * cols // n_dp, count * cols // n_dp)
+
     def scatter(c, slot_, peer):
         return pltpu.make_async_remote_copy(
-            src_ref=gsend.at[c, peer], dst_ref=rsbuf.at[c, slot_],
+            src_ref=gsend.at[rows_of(c, peer)], dst_ref=rsbuf.at[rows_of(c, slot_)],
             send_sem=r_send.at[c, peer], recv_sem=r_recv.at[c, slot_],
             device_id={"dp": peer}, device_id_type=MESH,
         )
 
     def spread_sum(c, slot_, peer):
         return pltpu.make_async_remote_copy(
-            src_ref=asend.at[c], dst_ref=grad.at[c, slot_],
+            src_ref=asend.at[sum_rows(c)], dst_ref=grad.at[rows_of(c, slot_)],
             send_sem=a_send.at[c, peer], recv_sem=a_recv.at[c, slot_],
             device_id={"dp": peer}, device_id_type=MESH,
         )
 
     def reduce(c):
-        total = gsend[c, dp].astype(jnp.float32)
+        total = gsend[rows_of(c, dp), :].astype(jnp.float32)
         for peer in dp_peers:
             scatter(c, peer, peer).wait_recv()
-            total = total + rsbuf[c, peer].astype(jnp.float32)
-        asend[c] = total.astype(jnp.bfloat16)
+            total = total + rsbuf[rows_of(c, peer), :].astype(jnp.float32)
+        total = total.astype(jnp.bfloat16)
+        asend[sum_rows(c), :] = total
         for peer in dp_peers:
             spread_sum(c, dp, peer).start()
-        grad[c, dp] = asend[c]
-
-    for c in range(chunks):
+        grad[rows_of(c, dp), :] = total
+
+    for c, (start, count) in enumerate(plan):
+        left, right = start * cols, (start + count) * cols
         for i, peer in enumerate(z_peers):
-            gather(c, peer, peer, i, rsend.at[c], g_send).wait_recv()
-            forward = gather(c, peer, sibling, i, gbuf.at[c, peer], f_send)
+            gather(c, peer, peer, i, held(c, peer), g_send).wait_recv()
+            forward = gather(c, peer, sibling, i, held(c, peer), f_send)
             forward.start()
             sends.append(forward)
-        gather(c, sibling, sibling, n_z - 1, rsend.at[c], g_send).wait_recv()
+        gather(c, sibling, sibling, n_z - 1, held(c, sibling), g_send).wait_recv()
         for i, peer in enumerate(f_peers):
-            gather(c, peer, sibling, i, rsend.at[c], f_send).wait_recv()
+            gather(c, peer, sibling, i, held(c, peer), f_send).wait_recv()
 
         def combine(b):
             at = b * SLOTS
-            found = gbuf[c, :, pl.ds(at, SLOTS), :].reshape(rows, cols)
-            comb[pl.ds(b * tok, tok), c * cols : (c + 1) * cols] = jnp.dot(
+            found = jnp.concatenate(
+                [
+                    gbuf[u, :, pl.ds(at, SLOTS), :].reshape(rows, cols)
+                    for u in range(start, start + count)
+                ],
+                axis=1,
+            )
+            comb[pl.ds(b * tok, tok), left:right] = jnp.dot(
                 weight[b], found, preferred_element_type=jnp.float32
             ).astype(jnp.bfloat16)
 
         each(n_e, combine)
         partial = lax.dot_general(
-            comb[:, c * cols : (c + 1) * cols], cot[...], (((0,), (0,)), ((), ())),
+            comb[:, left:right], cot[...], (((0,), (0,)), ((), ())),
             preferred_element_type=jnp.float32,
         )
-        gsend[c] = partial.astype(jnp.bfloat16).reshape(n_dp, share, cot.shape[1])
+        gsend[left:right, :] = partial.astype(jnp.bfloat16)
         for peer in dp_peers:
             scatter(c, dp, peer).start()
         if c > 0:
@@ -250,12 +277,12 @@
 def finish_kernel(mixed_ref, grad_ref, mixed_out, grad_out, wide, mixed_sem, grad_sem):
     copy = pltpu.make_async_copy(mixed_ref, mixed_out, mixed_sem)
     copy.start()
-    chunks, n_dp, share = grad_ref.shape[:3]
+    parts, deep = wide.shape[:2]
     outs = []
-    for c in range(chunks):
-        wide[c] = grad_ref[c].astype(jnp.float32).reshape(n_dp * share, grad_ref.shape[3])
-        at = pl.ds(c * n_dp * share, n_dp * share)
-        outs.append(pltpu.make_async_copy(wide.at[c], grad_out.at[at], grad_sem.at[c]))
+    for i in range(parts):
+        at = pl.ds(i * deep, deep)
+        wide[i] = grad_ref[at, :].astype(jnp.float32)
+        outs.append(pltpu.make_async_copy(wide.at[i], grad_out.at[at], grad_sem.at[i]))
         outs[-1].start()
     copy.wait()
     for out in outs:
@@ -263,7 +290,7 @@
 
 
 def finish(mixed, grad):
-    chunks, n_dp, share, features = grad.shape
+    parts, (width, features) = 4, grad.shape
     vmem = pl.BlockSpec(memory_space=pltpu.VMEM)
     hbm = pl.BlockSpec(memory_space=pl.ANY)
     dma = pltpu.SemaphoreType.DMA
@@ -271,14 +298,14 @@
         finish_kernel,
         out_shape=(
             jax.ShapeDtypeStruct(mixed.shape, mixed.dtype),
-            jax.ShapeDtypeStruct((chunks * n_dp * share, features), jnp.float32),
+            jax.ShapeDtypeStruct(grad.shape, jnp.float32),
         ),
         in_specs=[vmem, vmem],
         out_specs=(hbm, hbm),
         scratch_shapes=[
-            pltpu.VMEM((chunks, n_dp * share, features), jnp.float32),
+            pltpu.VMEM((parts, width // parts, features), jnp.float32),
             dma,
-            dma((chunks,)),
+            dma((parts,)),
         ],
         compiler_params=pltpu.CompilerParams(vmem_limit_bytes=50 * 1024 * 1024),
     )(mixed, grad)
@@ -288,9 +315,10 @@
     tok, width = latent.shape
     hidden = expert_out.shape[1]
     group, features = cotangent.shape
-    chunks = max(1, min(4, width // (16 * n_dp)))
-    cols = width // chunks
-    share = cols // n_dp
+    units = max(1, min(4, width // (16 * n_dp)))
+    cols = width // units
+    plan = [(0, 1), (1, 2), (3, 1)] if units == 4 else [(u, 1) for u in range(units)]
+    chunks = len(plan)
     rows = n_e * SLOTS
     n_z = n_e // CORES
     tall = message_rows(n_e, tok, width)
@@ -299,10 +327,10 @@
     bf16 = jnp.bfloat16
     dma = pltpu.SemaphoreType.DMA
     mixed, grad = pl.pallas_call(
-        functools.partial(kernel, n_e, n_dp, chunks),
+        functools.partial(kernel, n_e, n_dp, units, plan),
         out_shape=(
             pltpu.VMEM((group, features), bf16),
-            pltpu.VMEM((chunks, n_dp, share, features), bf16),
+            pltpu.VMEM((width, features), bf16),
         ),
         in_specs=[vmem, vmem, vmem, hbm, hbm, hbm, hbm],
         out_specs=(vmem, vmem),
@@ -314,13 +342,13 @@
             pltpu.VMEM((n_e, tall, width), bf16),
             pltpu.VMEM((n_e, tall, width), bf16),
             pltpu.VMEM((rows, hidden), bf16),
-            pltpu.VMEM((chunks, rows, cols), bf16),
-            pltpu.VMEM((chunks, n_e, rows, cols), bf16),
+            pltpu.VMEM((units, rows, cols), bf16),
+            pltpu.VMEM((units, n_e, rows, cols), bf16),
             pltpu.VMEM((n_e, tok, rows), bf16),
             pltpu.VMEM((group, width), bf16),
-            pltpu.VMEM((chunks, n_dp, share, features), bf16),
-            pltpu.VMEM((chunks, n_dp, share, features), bf16),
-            pltpu.VMEM((chunks, share, features), bf16),
+            pltpu.VMEM((width, features), bf16),
+            pltpu.VMEM((width, features), bf16),
+            pltpu.VMEM((width // n_dp, features), bf16),
             dma((4,)),
             dma((n_e,)),
             dma((n_e,)),

time: 38.1 us -> 40.4 us (1.060)
  Pallas kernels: 37.3 us -> 39.4 us
    pallas_call x1, Pallas kernels: 35.9 us -> 38 us  [body(): pl.pallas_call(functools.partial(kernel, n_e, n_dp, units, plan), out_sha...]
where the time goes in v7:
time: 40.4 us; the launch traced here: 40 us
  Pallas kernels  39.4 us (98%)
  between operations  0.64 us (2%)
    pallas_call x1, Pallas kernels, body(): pl.pallas_call(functools.partial(kernel, n_e, n_dp, units, plan), out_sha...  38 us
    pallas_call x1, Pallas kernels, finish(): pl.pallas_call(finish_kernel, out_shape=(jax.ShapeDtypeStruct(mixed.shape...  1.35 us

profile of v7, /device:TPU:0, one launch (start us, length us, event | category | flops | bytes accessed | tf_op | source)
XLA Modules:
  0.0 40.0 jit_solution(17508006942656590605)
XLA Ops:
  0.6 38.0 %shard_map.86 = (bf16[1024,512]{1,0:T(8,128)(2,1)S(1)}, bf16[512,512]{1,0:T(8,128)(2,1)S(1)}) custom-call(s32[8,128]{1,0:T(8,128)} %bitcast.2, bf16[8,128]{1,0:T(8,128)(2,1)} %bitcast.3, bf16[128,512]{1,0:T(8,128)(2,1)} %latent_ref.1, bf16[512,512]{1,0:T(8,128)(2,1)} %up_hbm.1, bf16[1,512,4096]{2,1,0:T(8,128)(2,1)} %win_hbm.1, ...), custom_call_target="tpu_custom_call" | custom-call | flops 1879048192 | bytes 10485760 | tf_op jit(solution)/shard_map/pallas_call | solution.py:329
  38.7 1.4 %shard_map.87 = (bf16[1024,512]{1,0:T(8,128)(2,1)}, f32[512,512]{1,0:T(8,128)}) custom-call(bf16[1024,512]{1,0:T(8,128)(2,1)S(1)} %get-tuple-element.4.mixed_ref, bf16[512,512]{1,0:T(8,128)(2,1)S(1)} %get-tuple-element.5.grad_ref), custom_call_target="tpu_custom_call" | custom-call | tf_op jit(solution)/shard_map/pallas_call | solution.py:297

commit v8 on v6

--- a/solution.py
+++ b/solution.py
@@ -171,29 +171,38 @@
     each(n_e, weigh)
     loads[2].wait()
 
-    def scatter(c, slot_, peer):
+    features = cot.shape[1]
+    splits = [2 if c == chunks - 1 and features % 256 == 0 else 1 for c in range(chunks)]
+
+    def lanes(c, p):
+        return pl.ds(p * (features // splits[c]), features // splits[c])
+
+    def scatter(c, p, slot_, peer):
         return pltpu.make_async_remote_copy(
-            src_ref=gsend.at[c, peer], dst_ref=rsbuf.at[c, slot_],
-            send_sem=r_send.at[c, peer], recv_sem=r_recv.at[c, slot_],
+            src_ref=gsend.at[c, peer, :, lanes(c, p)], dst_ref=rsbuf.at[c, slot_, :, lanes(c, p)],
+            send_sem=r_send.at[c + p, peer], recv_sem=r_recv.at[c + p, slot_],
             device_id={"dp": peer}, device_id_type=MESH,
         )
 
-    def spread_sum(c, slot_, peer):
+    def spread_sum(c, p, slot_, peer):
         return pltpu.make_async_remote_copy(
-            src_ref=asend.at[c], dst_ref=grad.at[c, slot_],
-            send_sem=a_send.at[c, peer], recv_sem=a_recv.at[c, slot_],
+            src_ref=asend.at[c, :, lanes(c, p)], dst_ref=grad.at[c, slot_, :, lanes(c, p)],
+            send_sem=a_send.at[c + p, peer], recv_sem=a_recv.at[c + p, slot_],
             device_id={"dp": peer}, device_id_type=MESH,
         )
 
     def reduce(c):
-        total = gsend[c, dp].astype(jnp.float32)
-        for peer in dp_peers:
-            scatter(c, peer, peer).wait_recv()
-            total = total + rsbuf[c, peer].astype(jnp.float32)
-        asend[c] = total.astype(jnp.bfloat16)
-        for peer in dp_peers:
-            spread_sum(c, dp, peer).start()
-        grad[c, dp] = asend[c]
+        for p in range(splits[c]):
+            at = lanes(c, p)
+            total = gsend[c, dp, :, at].astype(jnp.float32)
+            for peer in dp_peers:
+                scatter(c, p, peer, peer).wait_recv()
+                total = total + rsbuf[c, peer, :, at].astype(jnp.float32)
+            total = total.astype(jnp.bfloat16)
+            asend[c, :, at] = total
+            for peer in dp_peers:
+                spread_sum(c, p, dp, peer).start()
+            grad[c, dp, :, at] = total
 
     for c in range(chunks):
         for i, peer in enumerate(z_peers):
@@ -213,13 +222,17 @@
             ).astype(jnp.bfloat16)
 
         each(n_e, combine)
-        partial = lax.dot_general(
-            comb[:, c * cols : (c + 1) * cols], cot[...], (((0,), (0,)), ((), ())),
-            preferred_element_type=jnp.float32,
-        )
-        gsend[c] = partial.astype(jnp.bfloat16).reshape(n_dp, share, cot.shape[1])
-        for peer in dp_peers:
-            scatter(c, dp, peer).start()
+        for p in range(splits[c]):
+            at = lanes(c, p)
+            partial = lax.dot_general(
+                comb[:, c * cols : (c + 1) * cols], cot[:, at], (((0,), (0,)), ((), ())),
+                preferred_element_type=jnp.float32,
+            )
+            gsend[c, :, :, at] = partial.astype(jnp.bfloat16).reshape(
+                n_dp, share, features // splits[c]
+            )
+            for peer in dp_peers:
+                scatter(c, p, dp, peer).start()
         if c > 0:
             reduce(c - 1)
 
@@ -241,10 +254,11 @@
     for copy in sends:
         copy.wait_send()
     for c in range(chunks):
-        for peer in dp_peers:
-            scatter(c, dp, peer).wait_send()
-            spread_sum(c, dp, peer).wait_send()
-            spread_sum(c, peer, peer).wait_recv()
+        for p in range(splits[c]):
+            for peer in dp_peers:
+                scatter(c, p, dp, peer).wait_send()
+                spread_sum(c, p, dp, peer).wait_send()
+                spread_sum(c, p, peer, peer).wait_recv()
 
 
 def finish_kernel(mixed_ref, grad_ref, mixed_out, grad_out, wide, mixed_sem, grad_sem):
@@ -327,10 +341,10 @@
             dma((chunks, n_z)),
             dma((chunks, n_e)),
             dma((chunks, n_z)),
-            dma((chunks, n_dp)),
-            dma((chunks, n_dp)),
-            dma((chunks, n_dp)),
-            dma((chunks, n_dp)),
+            dma((chunks + 1, n_dp)),
+            dma((chunks + 1, n_dp)),
+            dma((chunks + 1, n_dp)),
+            dma((chunks + 1, n_dp)),
         ],
         compiler_params=pltpu.CompilerParams(
             collective_id=0, has_side_effects=True, vmem_limit_bytes=54 * 1024 * 1024

time: 38.1 us -> 37.9 us (level)
  no operation moved by 1% of the time
where the time goes in v8:
time: 37.9 us; the launch traced here: 37.8 us
  Pallas kernels  37.1 us (98%)
  between operations  0.64 us (2%)
    pallas_call x1, Pallas kernels, body(): pl.pallas_call(functools.partial(kernel, n_e, n_dp, chunks), out_shape=(p...  35.8 us
    pallas_call x1, Pallas kernels, finish(): pl.pallas_call(finish_kernel, out_shape=(jax.ShapeDtypeStruct(mixed.shape...  1.35 us

profile of v8, /device:TPU:0, one launch (start us, length us, event | category | flops | bytes accessed | tf_op | source)
XLA Modules:
  0.0 37.8 jit_solution(1211368749294007324)
XLA Ops:
  0.6 35.8 %shard_map.86 = (bf16[1024,512]{1,0:T(8,128)(2,1)S(1)}, bf16[4,4,32,512]{3,2,1,0:T(8,128)(2,1)S(1)}) custom-call(s32[8,128]{1,0:T(8,128)} %bitcast.2, bf16[8,128]{1,0:T(8,128)(2,1)} %bitcast.3, bf16[128,512]{1,0:T(8,128)(2,1)} %latent_ref.1, bf16[512,512]{1,0:T(8,128)(2,1)} %up_hbm.1, bf16[1,512,4096]{2,1,0:T(8,128)(2,1)} %win_hbm.1, ...), custom_call_target="tpu_custom_call" | custom-call | flops 1879048192 | bytes 10485760 | tf_op jit(solution)/shard_map/pallas_call | solution.py:315
  36.4 1.4 %shard_map.87 = (bf16[1024,512]{1,0:T(8,128)(2,1)}, f32[512,512]{1,0:T(8,128)}) custom-call(bf16[1024,512]{1,0:T(8,128)(2,1)S(1)} %get-tuple-element.4.mixed_ref, bf16[4,4,32,512]{3,2,1,0:T(8,128)(2,1)S(1)} %get-tuple-element.5.grad_ref), custom_call_target="tpu_custom_call" | custom-call | tf_op jit(solution)/shard_map/pallas_call | solution.py:284
